TPU v7x, 256 devices: a whole 4x4x8 slice. The times are simulated.
256 devices in a mesh: seq: 16 (over y_lo, z), tensor: 16 (over y_hi, x, core).
Axes of the slice: x: 4, y: 4 (y_hi: 2, y_lo: 2; y = y_hi * 2 + y_lo), z: 8, core: 2. Of those that a mesh axis runs over, the one named last changes fastest.
Arguments:
- teacher_hidden: bfloat16 [2048, 16384], P('seq', 'tensor'), may hold values from -400 to 400
- teacher_gain: float32 [16384], P('tensor'), may hold values from 0.1 to 1.9
- projector: bfloat16 [16384, 8192], P('tensor', 'seq'), may hold values from -0.0625 to 0.0625
- student_hidden: bfloat16 [2048, 8192], P('seq', 'tensor'), may hold values from -20 to 20
- student_gain: float32 [8192], P('tensor'), may hold values from 0.1 to 1.9
- query_weight: bfloat16 [8192, 4096], P(None, 'tensor'), may hold values from -0.6 to 0.6
- kv_weight: bfloat16 [2, 8192, 512], P(None, None, 'tensor'), may hold values from -0.6 to 0.6
- out_weight: bfloat16 [4096, 8192], P('tensor'), may hold values from -0.125 to 0.125
- doc_ids: int32 [2048], P('seq'), may hold values from 0 to 7, never falling along the last dimension, each value on 1 to 1024 neighbouring positions
Outputs:
- student_out: bfloat16 [2048, 8192], P('seq', 'tensor')
- loss_rows: float32 [2048], P('seq')
- grad_attn: bfloat16 [2048, 4096], P('seq', 'tensor')
Inputs may be any that keep to these rules, and one draw needn't show every extreme that they name: `doc_ids`: each document's positions are consecutive and ids never fall; a document holds at most 1024 positions.
All inputs are finite; a program needn't handle non-finite values.
Results may differ from a plain program's by a relative error of at most 0.03.
The roundings to bfloat16 on the way count: a program that leaves them out, or rounds other values in their place, can miss the bound.
Values may be sent and summed in bfloat16 or wider, within the bound.
A program may use at most 128 MiB of HBM per device.

v0:
```python
import math

import jax
import jax.numpy as jnp
from jax import lax
from jax.experimental import pallas as pl
from jax.experimental.pallas import tpu as pltpu
from jax.sharding import PartitionSpec as P

DT = 16384
DS = 8192
HEAD_DIM = 128
HEADS = 32
KV_HEADS = 4
ROWS = 128
COLS = 512
BACK = 8
F32 = jnp.float32
BF16 = jnp.bfloat16
MESH = pl.DeviceIdType.MESH
NT = (((1,), (1,)), ((), ()))


def nt_dot(a, b):
    return lax.dot_general(a, b, NT, preferred_element_type=F32)


def body(
    th_h, tgain_h, pj_h, sh_h, sgain_h, wq_h, wkv_h, wo_h, docs_h,
    out_s, out_l, out_g,
    tgain, sgain, docs, th_v, tg, pj, wq, wkv, wo, cos_t, sin_t,
    hb, sg_s, sg_r, sum_s, sum_r, scale_v, q_acc, q_in, kv_acc, kv_in,
    kvx_s, kvx_r, kv_own, kv_r, docs_z, docs_o, q_v, attn_v, bias,
    t_own, t_part, o_own, o_x2, t_sib_s, t_sib_r, t_x2, t_ra, t_rb, t_xp, t_xm, t_fm, t_fp, t_ys, t_yr, t_fin,
    o_ra, o_rb, o_xp, o_xm, o_fm, o_fp, o_ys, o_yr, o_fin,
    t3_s, t3_r, ts_v, db, g_acc, g_in, l_v, l_s, l_r,
    load_sem, w_load, w_ss, w_rs, v_load, v_ss, v_rs, u_ss, u_rs, x_ss, x_rs, z_ss, z_rs, p_ss, p_rs,
    ag_ss, ag_rs, dg_ss, dg_rs, sm_ss, sm_rs, kx_ss, kx_rs, kv_ss, kv_rs, kf_ss, kf_rs, dc_ss, dc_rs,
    t_ss, t_rs, o_ss, o_rs, t3_ss, t3_rs, l_ss, l_rs,
):
    s = lax.axis_index("seq")
    t = lax.axis_index("tensor")
    yl, z = s // 8, s % 8
    yh, x, c = t // 8, (t // 2) % 4, t % 2

    def tid(y_, x_, c_):
        return y_ * 8 + x_ * 2 + c_

    xp_, xm_ = (x + 1) % 4, (x + 3) % 4
    xf_ = (x + 2) % 4
    yo_ = 1 - yh
    sib = (s, tid(yh, x, 1 - c))
    dev_xp = (s, tid(yh, xp_, c))
    dev_xm = (s, tid(yh, xm_, c))
    dev_yo = (s, tid(yo_, x, c))
    dev_zp = (yl * 8 + (z + 1) % 8, t)
    dev_zm = (yl * 8 + (z + 7) % 8, t)
    dev_yl = ((1 - yl) * 8 + z, t)
    turn = jnp.where(c == 0, x, jnp.where(x == 0, 4, 8 - x))
    dev_t3 = (yl * 8 + (z + turn) % 8, yh * 8 + z)
    stays = (z == 0) & (x == 0) & (c == 0)

    started = []

    def copy(src, dst, ss, rs, dev):
        return pltpu.make_async_remote_copy(
            src_ref=src, dst_ref=dst, send_sem=ss, recv_sem=rs, device_id=dev, device_id_type=MESH
        )

    def send(src, dst, ss, rs, dev):
        one = copy(src, dst, ss, rs, dev)
        one.start()
        started.append(one)

    def flush():
        for one in started:
            one.wait_send()
        started.clear()

    def arrive(dst, ss, rs):
        copy(dst, dst, ss, rs, sib).wait_recv()

    def load(src, dst, k):
        one = pltpu.make_async_copy(src, dst, load_sem.at[k])
        one.start()
        return one

    l_th = load(th_h, th_v, 0)
    mine = yh * 4 + x
    l_sh = load(sh_h, hb.at[mine], 1)
    l_small = [load(tgain_h, tgain, 7), load(sgain_h, sgain, 8), load(docs_h, docs, 9)]

    def wkv_part(j, core):
        return wkv_h.at[:, :, pl.ds(pl.multiple_of((j * 2 + core) * COLS, COLS), COLS)]

    def wkv_load(j):
        return pltpu.make_async_copy(wkv_part(j, c), wkv.at[j, c], v_load.at[j])

    def wkv_go(j, carry):
        wkv_load(j).start()
        return carry

    def wo_part(j, core):
        return wo_h.at[:, pl.ds(pl.multiple_of((j * 2 + core) * COLS, COLS), COLS)]

    def wo_load(j):
        return pltpu.make_async_copy(wo_part(j, c), wo.at[j, c], w_load.at[j])

    def wo_send(j):
        return copy(wo_part(j, 1 - c), wo.at[j, c], w_ss.at[j], w_rs.at[j], sib)

    def wo_fetch(j, carry):
        wo_load(j).start()
        return carry

    def wo_go(j, carry):
        wo_send(j).start()
        return carry

    def wo_got(j, carry):
        wo_load(j).wait()
        arrive(wo.at[j, 1 - c], w_ss.at[j], w_rs.at[j])
        return carry

    def wo_end(j, carry):
        wo_send(j).wait_send()
        return carry

    kv_r[...] = jnp.zeros(kv_r.shape, BF16)

    barrier = pltpu.get_barrier_semaphore()
    for dev in (sib, dev_xp, dev_xm, dev_yo, dev_zp, dev_zm, dev_yl):
        pl.semaphore_signal(barrier, inc=1, device_id=dev, device_id_type=MESH)

    class Gather:
        def __init__(self, buf, ss, rs):
            self.buf, self.ss, self.rs = buf, ss, rs
            self.near = [yh * 4 + xm_, yh * 4 + xp_]
            self.opp = yo_ * 4 + x
            self.onear = [yo_ * 4 + xm_, yo_ * 4 + xp_]
            self.far = [yh * 4 + xf_, yo_ * 4 + xf_]
            self.order = [mine] + self.near + [self.opp] + self.onear + self.far

        def part(self, slot, h):
            return self.buf.at[slot, pl.ds(h * 64, 64)]

        def half(self, slot, h, k, dev):
            part = self.part(slot, h)
            send(part, part, self.ss.at[k], self.rs.at[k], dev)

        def got_half(self, slot, h, k):
            arrive(self.part(slot, h), self.ss.at[k], self.rs.at[k])

        def begin(self, h):
            self.half(mine, h, 0 + h, dev_yo)
            self.half(mine, h, 2 + h, dev_xp)
            self.half(mine, h, 4 + h, dev_xm)

        def near_relay(self):
            self.got_half(self.near[0], 0, 2)
            self.half(self.near[0], 0, 6, dev_xp)
            self.got_half(self.near[1], 1, 5)
            self.half(self.near[1], 1, 7, dev_xm)

        def near_rest(self):
            self.got_half(self.near[0], 1, 3)
            self.got_half(self.near[1], 0, 4)

        def opp_half(self, h):
            self.got_half(self.opp, h, 0 + h)
            self.half(self.opp, h, 8 + h, dev_xp)
            self.half(self.opp, h, 10 + h, dev_xm)

        def onear_a(self):
            self.got_half(self.onear[0], 0, 8)
            self.half(self.onear[0], 0, 12, dev_xp)

        def onear_b(self):
            self.got_half(self.onear[1], 1, 11)
            self.half(self.onear[1], 1, 13, dev_xm)

        def onear_rest(self):
            self.got_half(self.onear[0], 1, 9)
            self.got_half(self.onear[1], 0, 10)

        def far_step(self):
            self.got_half(self.far[0], 0, 6)
            self.got_half(self.far[0], 1, 7)

        def ofar_step(self):
            self.got_half(self.far[1], 0, 12)
            self.got_half(self.far[1], 1, 13)

    def pj_send(k):
        rows = pl.ds(k * 128, 128)
        send(pj_h.at[rows], pj.at[yl, rows], p_ss.at[k], p_rs.at[k], dev_yl)

    def wkv_send(j):
        return copy(wkv_part(j, 1 - c), wkv.at[j, c], v_ss.at[j], v_rs.at[j], sib)

    def wq_send(j):
        return copy(wq_h.at[j, 1 - c], wq.at[j, c], u_ss.at[j], u_rs.at[j], sib)

    def w_go(j, carry):
        wkv_send(j).start()
        wq_send(j).start()
        return carry

    def w_end(j, carry):
        wkv_send(j).wait_send()
        wq_send(j).wait_send()
        return carry

    def w_got(slot):
        wkv_load(slot).wait()
        arrive(wkv.at[slot, 1 - c], v_ss.at[slot], v_rs.at[slot])
        arrive(wq.at[slot, 1 - c], u_ss.at[slot], u_rs.at[slot])

    ag = Gather(hb, ag_ss, ag_rs)
    l_sh.wait()
    pl.semaphore_wait(barrier, 7)
    ag.begin(0)

    z_slot = 0
    l_th.wait()
    for one in l_small:
        one.wait()
    docs_z[z] = docs[...]
    part = jnp.zeros((ROWS, 128), F32)
    for i in range(8):
        cols = slice(i * 128, (i + 1) * 128)
        f = th_v[:, cols].astype(F32)
        part = part + f * f
        tg[z_slot, :, cols] = (f * tgain[:, cols]).astype(BF16)
    sg_s[:, COLS:COLS + 128] = jnp.sum(part.T, axis=0, keepdims=True)
    part = jnp.zeros((ROWS, 128), F32)
    for i in range(4):
        f = hb[mine, :, i * 128:(i + 1) * 128].astype(F32)
        part = part + f * f
    sg_s[:, COLS + 128:COLS + 256] = jnp.sum(part.T, axis=0, keepdims=True)
    sg_s[:, 0:COLS] = sgain[...]
    sg_r[mine] = sg_s[...]

    def ring_slot(d):
        return (0, 1, 2, 3, 4, 7, 6, 5)[d % 8]

    def z_ref(d, h):
        return tg.at[ring_slot(d), pl.ds(h * 64, 64)]

    def z_send(k):
        d = k // 2
        send(z_ref(8 - d, k % 2), z_ref(7 - d, k % 2), z_ss.at[k], z_rs.at[k], dev_zp)
        send(z_ref(d, 1 - k % 2), z_ref(d + 1, 1 - k % 2), z_ss.at[8 + k], z_rs.at[8 + k], dev_zm)

    def z_got(k):
        up, down = z_ref(-(k // 2) + 7, k % 2), z_ref(k // 2 + 1, 1 - k % 2)
        arrive(up, z_ss.at[k], z_rs.at[k])
        arrive(down, z_ss.at[8 + k], z_rs.at[8 + k])

    def z_step(k):
        z_got(k)
        if k + 2 < 7:
            z_send(k + 2)

    def small_send(i, k, dev):
        slot = ag.order[i]
        send(sg_r.at[slot], sg_r.at[slot], sm_ss.at[k], sm_rs.at[k], dev)

    def small_got(i, k):
        arrive(sg_r.at[ag.order[i]], sm_ss.at[k], sm_rs.at[k])

    def docs_send(d, k, dev):
        ref = docs_z.at[(z + d) % 8]
        send(ref, ref, dc_ss.at[k], dc_rs.at[k], dev)

    def docs_step(k):
        arrive(docs_z.at[(z + 7 - k) % 8], dc_ss.at[k], dc_rs.at[k])
        if k < 3:
            arrive(docs_z.at[(z + 1 + k) % 8], dc_ss.at[4 + k], dc_rs.at[4 + k])
            docs_send(7 - k, k + 1, dev_zp)
            if k < 2:
                docs_send(1 + k, k + 5, dev_zm)
        else:
            send(docs_z, docs_o, dc_ss.at[8], dc_rs.at[8], dev_yl)

    small_send(0, 0, dev_yo)
    small_send(0, 1, dev_xp)
    small_send(0, 2, dev_xm)
    ag.begin(1)
    docs_send(0, 0, dev_zp)
    docs_send(0, 4, dev_zm)
    z_send(0)
    pj_send(0)
    lax.fori_loop(0, 8, wkv_go, 0)
    l_wq = load(wq_h.at[:, c], wq.at[:, c], 3)
    lax.fori_loop(0, 8, w_go, 0)
    z_send(1)
    l_pj = load(pj_h, pj.at[yl], 4)

    entry = lax.broadcasted_iota(jnp.int32, (64, ROWS), 0).astype(F32)
    position = (s * ROWS + lax.broadcasted_iota(jnp.int32, (64, ROWS), 1)).astype(F32)
    angle = position * jnp.exp(-math.log(500000.0) * (2.0 * entry / HEAD_DIM))
    cos_t[...] = jnp.cos(angle)
    sin_t[...] = jnp.sin(angle)

    def process(slots, first=False):
        blocks, w = [], []
        for slot in slots:
            parts = []
            for i in range(4):
                cols = slice(i * 128, (i + 1) * 128)
                f = hb[slot, :, cols].astype(F32)
                parts.append((f * scale_v[...] * sg_r[slot][:, cols]).astype(BF16))
            blocks.append(jnp.concatenate(parts, axis=1))
        n = jnp.concatenate(blocks, axis=1)
        for slot in slots:
            w_got(slot)
            w.append(wkv[slot].reshape(128, COLS))
        kv = nt_dot(jnp.concatenate(w, axis=1), n)
        for core in range(2):
            w = jnp.concatenate([wq[slot, core] for slot in slots], axis=0)
            q = jnp.dot(n, w, preferred_element_type=F32)
            k = kv[core * 64:core * 64 + 64]
            q_acc[core] = q if first else q_acc[core] + q
            kv_acc[core] = k if first else kv_acc[core] + k

    small_got(1, 1)
    small_send(1, 3, dev_xp)
    small_got(2, 2)
    small_got(3, 0)
    small_send(3, 4, dev_xp)
    small_send(3, 5, dev_xm)
    docs_step(0)
    ag.near_relay()
    pj_send(1)
    small_got(6, 3)
    docs_step(1)
    small_got(4, 4)
    small_send(4, 6, dev_xp)
    small_got(5, 5)
    ag.near_rest()
    ag.opp_half(0)
    z_step(0)
    pj_send(2)
    small_got(7, 6)
    sums = sg_r[0][:, COLS:COLS + 256]
    for i in range(1, 8):
        sums = sums + sg_r[i][:, COLS:COLS + 256]
    sum_s[...] = sums
    send(sum_s, sum_r, x_ss.at[2], x_rs.at[2], sib)
    docs_step(2)
    ag.opp_half(1)
    pj_send(3)
    arrive(sum_r, x_ss.at[2], x_rs.at[2])
    sums = sum_s[...] + sum_r[...]
    ts_v[...] = jnp.broadcast_to(lax.rsqrt(sums[:, 0:128] / DT + 1e-05), (ROWS, 128)).T
    scale_v[...] = jnp.broadcast_to(lax.rsqrt(sums[:, 128:256] / DS + 1e-05), (ROWS, 128)).T
    docs_step(3)
    z_step(1)
    ag.onear_a()
    pj_send(4)
    l_wq.wait()
    process([mine] + ag.near, True)
    ag.onear_b()
    pj_send(5)
    z_step(2)
    ag.far_step()
    process([ag.opp, ag.far[0]])
    pj_send(6)
    ag.onear_rest()
    process(ag.onear)
    pj_send(7)
    z_step(3)
    ag.ofar_step()
    process([ag.far[1]])
    send(kv_acc.at[1 - c], kv_in, x_ss.at[3], x_rs.at[3], sib)
    send(q_acc.at[1 - c], q_in, x_ss.at[4], x_rs.at[4], sib)
    arrive(kv_in, x_ss.at[3], x_rs.at[3])

    row = lax.broadcasted_iota(jnp.int32, (64, 64), 0)
    col = lax.broadcasted_iota(jnp.int32, (64, 64), 1)
    take = ((row >> 3) & 1) * 32 + (row & 7) * 4 + (row >> 4)
    pick = jnp.where(col == take, 1.0, 0.0).astype(BF16)
    kv_mine = (kv_acc[c] + kv_in[...]).astype(BF16)
    kvx_s[...] = jnp.dot(pick, kv_mine, preferred_element_type=F32).astype(BF16).reshape(4, 16, 128)
    kvx_r[t] = kvx_s[t // 4]

    def kvx(k):
        to = (t + k) % 16
        return copy(kvx_s.at[to // 4], kvx_r.at[t], kx_ss.at[k], kx_rs.at[k], (s, to))

    def kvx_go(k, carry):
        kvx(k).start()
        return carry

    def kvx_got(k, carry):
        arrive(kvx_r.at[(t + 16 - k) % 16], kx_ss.at[k], kx_rs.at[k])
        return carry

    def kvx_end(k, carry):
        kvx(k).wait_send()
        return carry

    lax.fori_loop(1, 16, kvx_go, 0)
    z_step(4)

    cos2 = jnp.concatenate([cos_t[...], cos_t[...]], axis=0).T
    sin2 = jnp.concatenate([-sin_t[...], sin_t[...]], axis=0).T
    arrive(q_in, x_ss.at[4], x_rs.at[4])
    q_mine = q_acc[c] + q_in[...]
    for h in range(2):
        qh = q_mine[:, h * 128:(h + 1) * 128]
        turned = qh * cos2 + pltpu.roll(qh, 64, 1) * sin2
        q_v[h] = (turned * HEAD_DIM ** (-0.5)).astype(BF16)

    lax.fori_loop(1, 16, kvx_got, 0)
    both = kvx_r[...].astype(F32).reshape(16, 2, 8, ROWS)
    k_raw = both[:, 0].reshape(HEAD_DIM, ROWS)
    v_raw = both[:, 1].reshape(HEAD_DIM, ROWS)
    first, second = k_raw[0:64], k_raw[64:128]
    k_rot = jnp.concatenate(
        [first * cos_t[...] - second * sin_t[...], second * cos_t[...] + first * sin_t[...]], axis=0
    )
    kv_own[0] = k_rot.astype(BF16)
    kv_own[1] = v_raw.T.astype(BF16)
    kv_r[0, 0] = kv_own[0]
    kv_r[1, 0] = kv_own[1]

    def kv_copy(k):
        return copy(kv_own.at[c], kv_r.at[c, k], kv_ss.at[k], kv_rs.at[k], ((s + k) % 16, t))

    def kv_fwd(k):
        return copy(kv_r.at[c, k], kv_r.at[c, k], kf_ss.at[k], kf_rs.at[k], sib)

    def kv_go(k):
        @pl.when(s + k < 16)
        def _():
            kv_copy(k).start()

    def kv_mid(k):
        @pl.when(s >= k)
        def _():
            arrive(kv_r.at[c, k], kv_ss.at[k], kv_rs.at[k])
            kv_fwd(k).start()

    def kv_got(k, carry):
        @pl.when(s >= k)
        def _():
            arrive(kv_r.at[1 - c, k], kf_ss.at[k], kf_rs.at[k])
        return carry

    def kv_end(k, carry):
        @pl.when(s >= k)
        def _():
            kv_fwd(k).wait_send()

        @pl.when(s + k < 16)
        def _():
            kv_copy(k).wait_send()
        return carry

    arrive(docs_o, dc_ss.at[8], dc_rs.at[8])
    for k in range(1, BACK + 1):
        kv_go(k)

    def docs_back(j):
        at = (z + 8 - j) % 8
        return jnp.where(z >= j, docs_z[at], jnp.where(yl == 1, docs_o[at], -1))

    key_doc = jnp.concatenate([docs_back(j) for j in range(BACK + 1)], axis=1)
    row_doc = jnp.broadcast_to(docs[...].astype(F32), (ROWS, ROWS)).T[:, 0:1].astype(jnp.int32)
    wide = (ROWS, (BACK + 1) * ROWS)
    row_at = lax.broadcasted_iota(jnp.int32, wide, 0)
    key_at = lax.broadcasted_iota(jnp.int32, wide, 1)
    allowed = (key_doc == row_doc) & ((key_at >= ROWS) | (key_at <= row_at))
    bias[...] = jnp.where(allowed, 0.0, -1e30)

    class Reduce:
        def __init__(self, y_order, own, sib_s, sib_r, x2, ra, rb, xp, xm, fm, fp, ys, yr, fin, ss, rs):
            self.own, self.sib_s, self.sib_r = own, sib_s, sib_r
            self.x2, self.ra, self.rb, self.xp, self.xm, self.fm, self.fp = x2, ra, rb, xp, xm, fm, fp
            self.ys, self.yr, self.fin, self.ss, self.rs = ys, yr, fin, ss, rs
            self.y_order = y_order
            self.x_order = (xf_, xp_, xm_, x)

        def go(self, src, dst, k, dev):
            send(src, dst, self.ss.at[k], self.rs.at[k], dev)

        def got(self, dst, k):
            arrive(dst, self.ss.at[k], self.rs.at[k])

        def slot(self, k, i):
            return self.y_order[i] * 4 + self.x_order[k]

        def to_sib(self, k, i):
            slot = self.slot(k, i)
            self.go(self.sib_s.at[slot], self.sib_r.at[slot], k * 2 + i, sib)

        def sib_got(self, k, i):
            if self.sib_r is not None:
                self.got(self.sib_r.at[self.slot(k, i)], k * 2 + i)

        def pair(self, k, i, h):
            slot, rows = self.slot(k, i), slice(h * 64, h * 64 + 64)
            value = self.own[slot, rows]
            return value if self.sib_r is None else value + self.sib_r[slot, rows].astype(F32)

        def far(self, i):
            self.sib_got(0, i)
            self.x2[i, 0:64] = self.pair(0, i, 0).astype(BF16)
            self.go(self.x2.at[i, pl.ds(0, 64)], self.ra.at[i], 8 + i, dev_xp)
            self.x2[i, 64:128] = self.pair(0, i, 1).astype(BF16)
            self.go(self.x2.at[i, pl.ds(64, 64)], self.rb.at[i], 10 + i, dev_xm)

        def near(self, i):
            self.sib_got(1, i)
            self.xp[i, 64:128] = self.pair(1, i, 1).astype(BF16)
            self.go(self.xp.at[i, pl.ds(64, 64)], self.fm.at[i, pl.ds(64, 64)], 12 + i, dev_xp)
            self.sib_got(2, i)
            self.xm[i, 0:64] = self.pair(2, i, 0).astype(BF16)
            self.go(self.xm.at[i, pl.ds(0, 64)], self.fp.at[i, pl.ds(0, 64)], 14 + i, dev_xm)

        def relay(self, i):
            self.got(self.ra.at[i], 8 + i)
            self.xp[i, 0:64] = (self.pair(1, i, 0) + self.ra[i].astype(F32)).astype(BF16)
            self.go(self.xp.at[i, pl.ds(0, 64)], self.fm.at[i, pl.ds(0, 64)], 16 + i, dev_xp)
            self.got(self.rb.at[i], 10 + i)
            self.xm[i, 64:128] = (self.pair(2, i, 1) + self.rb[i].astype(F32)).astype(BF16)
            self.go(self.xm.at[i, pl.ds(64, 64)], self.fp.at[i, pl.ds(64, 64)], 18 + i, dev_xm)

        def join(self, i, h):
            rows, at = slice(h * 64, h * 64 + 64), pl.ds(h * 64, 64)
            if h == 0:
                self.sib_got(3, i)
            self.got(self.fm.at[i, at], (16, 12)[h] + i)
            self.got(self.fp.at[i, at], (14, 18)[h] + i)
            return self.pair(3, i, h) + self.fm[i, rows].astype(F32) + self.fp[i, rows].astype(F32)

        def join_one(self, i):
            mine = self.y_order[i] == yh
            for h in range(2):
                rows = slice(h * 64, h * 64 + 64)
                value = self.join(i, h)

                @pl.when(mine)
                def _():
                    self.fin[rows] = value

                @pl.when(jnp.logical_not(mine))
                def _():
                    self.ys[rows] = value.astype(BF16)
                    self.to_opp(h).start()

        def to_opp(self, h):
            at = pl.ds(h * 64, 64)
            return copy(self.ys.at[at], self.yr.at[at], self.ss.at[20 + h], self.rs.at[20 + h], dev_yo)

        def join_other(self):
            for h in range(2):
                self.ys[h * 64:h * 64 + 64] = self.join(0, h).astype(BF16)
                self.to_opp(h).start()

        def join_mine(self):
            for h in range(2):
                self.fin[h * 64:h * 64 + 64] = self.join(1, h)

        def end(self):
            for h in range(2):
                self.to_opp(h).wait_send()

        def last(self, h):
            rows = slice(h * 64, h * 64 + 64)
            self.got(self.yr.at[pl.ds(h * 64, 64)], 20 + h)
            return self.fin[rows] + self.yr[rows].astype(F32)

    rt = Reduce((yl, 1 - yl), t_own, t_sib_s, t_sib_r, t_x2, t_ra, t_rb, t_xp, t_xm, t_fm, t_fp, t_ys, t_yr, t_fin, t_ss, t_rs)

    z_step(5)
    z_step(6)

    def products(core, y_, k, width):
        rows = tg[pl.ds(core * 4, 4), :, k * width:(k + 1) * width].reshape(4 * ROWS, width)
        return jnp.dot(rows, pj[y_, k * width:(k + 1) * width], preferred_element_type=F32).reshape(4, ROWS, COLS)

    l_pj.wait()
    first = pl.ds(yl * 4, 4)
    t_sib_s[first] = products(1 - c, yl, 0, 1024).astype(BF16)
    for k in range(4):
        rt.to_sib(k, 0)
    t_own[first] = products(c, yl, 0, 1024)
    rt.far(0)
    rt.near(0)
    lax.fori_loop(0, 8, wo_fetch, 0)
    lax.fori_loop(0, 8, wo_go, 0)

    other = pl.ds((1 - yl) * 4, 4)
    for k in range(4):
        for part in (2 * k, 2 * k + 1):
            arrive(pj.at[1 - yl, pl.ds(part * 128, 128)], p_ss.at[part], p_rs.at[part])
        theirs = products(1 - c, 1 - yl, k, 256)
        if k == 0:
            t_part[...] = theirs
        elif k < 3:
            t_part[...] += theirs
        else:
            t_sib_s[other] = (t_part[...] + theirs).astype(BF16)
            for j in range(4):
                rt.to_sib(j, 1)
        if k == 0:
            t_own[other] = products(c, 1 - yl, k, 256)
        else:
            t_own[other] += products(c, 1 - yl, k, 256)
        if k == 1:
            rt.relay(0)
    rt.far(1)
    rt.near(1)
    rt.join_one(0)
    for k in (1, 2, 3, 4):
        kv_mid(k)
    rt.relay(1)
    for k in (5, 6, 7, 8):
        kv_mid(k)

    lax.fori_loop(1, BACK + 1, kv_got, 0)
    keys = jnp.concatenate([kv_r[0, j] for j in range(BACK + 1)], axis=1)
    values = kv_r[1].reshape((BACK + 1) * ROWS, HEAD_DIM)
    for h in range(2):
        scores = jnp.dot(q_v[h], keys, preferred_element_type=F32)
        scores = scores + bias[...]
        probs = jnp.exp(scores - jnp.max(scores, axis=1, keepdims=True))
        total = jnp.sum(probs, axis=1, keepdims=True)
        acc = jnp.dot(probs.astype(BF16), values, preferred_element_type=F32)
        attn_v[c * 2 + h] = (acc / total).astype(BF16)
        send(attn_v.at[c * 2 + h], attn_v.at[c * 2 + h], x_ss.at[5 + h], x_rs.at[5 + h], sib)
    lax.fori_loop(0, 8, wo_got, 0)

    ro = Reduce((yo_, yh), o_own, None, None, o_x2, o_ra, o_rb, o_xp, o_xm, o_fm, o_fp, o_ys, o_yr, o_fin, o_ss, o_rs)

    for h in range(2):
        arrive(attn_v.at[2 - 2 * c + h], x_ss.at[5 + h], x_rs.at[5 + h])
    attn = jnp.concatenate([attn_v[i] for i in range(4)], axis=1)

    def out_block(k, i):
        slot = ro.slot(k, i)
        o_own[slot] = jnp.dot(attn, wo[slot].reshape(COLS, COLS), preferred_element_type=F32)

    out_block(0, 0)
    ro.far(0)
    rt.join_one(1)
    out_block(1, 0)
    out_block(2, 0)
    ro.near(0)
    out_block(0, 1)
    ro.relay(0)
    ro.far(1)
    out_block(1, 1)
    out_block(2, 1)
    ro.near(1)
    out_block(3, 0)
    out_block(3, 1)
    ro.relay(1)

    def t3(h):
        at = pl.ds(h * 64, 64)
        return copy(t3_s.at[at], t3_r.at[at], t3_ss.at[h], t3_rs.at[h], dev_t3)

    for h in range(2):
        rows = slice(h * 64, h * 64 + 64)
        t3_s[rows] = rt.last(h).astype(BF16)

        @pl.when(stays)
        def _():
            t3_r[rows] = t3_s[rows]

        @pl.when(jnp.logical_not(stays))
        def _():
            t3(h).start()

    ro.join_other()
    ro.join_mine()

    def before_end():
        flush()
        lax.fori_loop(0, 8, w_end, 0)
        lax.fori_loop(0, 8, wo_end, 0)
        lax.fori_loop(1, 16, kvx_end, 0)
        lax.fori_loop(1, BACK + 1, kv_end, 0)
        rt.end()
        ro.end()

        @pl.when(jnp.logical_not(stays))
        def _():
            t3(0).wait_send()
            t3(1).wait_send()

    dg = Gather(db, dg_ss, dg_rs)
    for h in range(2):
        rows = slice(h * 64, h * 64 + 64)
        mixed = hb[mine, rows].astype(F32) + ro.last(h)
        out_s[rows] = mixed.astype(BF16)

        @pl.when(jnp.logical_not(stays))
        def _():
            arrive(t3_r.at[pl.ds(h * 64, 64)], t3_ss.at[h], t3_rs.at[h])

        target = t3_r[rows].astype(F32) * jnp.concatenate([ts_v[rows]] * 4, axis=1)
        difference = mixed - target
        db[mine, rows] = difference.astype(BF16)
        dg.begin(h)
        squares = difference * difference
        l_v[rows] = (
            squares[:, 0:128] + squares[:, 128:256] + squares[:, 256:384] + squares[:, 384:512]
        )
    l_s[...] = jnp.sum(l_v[...].T, axis=0, keepdims=True)
    l_r[t] = l_s[...]

    def loss(k):
        return copy(l_s, l_r.at[t], l_ss.at[k], l_rs.at[k], (s, (t + k) % 16))

    def loss_go(k, carry):
        loss(k).start()
        return carry

    def loss_got(k, carry):
        arrive(l_r.at[(t + 16 - k) % 16], l_ss.at[k], l_rs.at[k])
        return carry

    def loss_end(k, carry):
        loss(k).wait_send()
        return carry

    lax.fori_loop(1, 16, loss_go, 0)

    def add_grad(slots, first=False):
        d = jnp.concatenate([db[slot] for slot in slots], axis=1)
        for core in range(2):
            w = jnp.concatenate([wo[slot, core] for slot in slots], axis=1)
            g = nt_dot(d, w)
            g_acc[core] = g if first else g_acc[core] + g

    dg.near_relay()
    dg.opp_half(0)
    dg.near_rest()
    before_end()
    add_grad([mine] + dg.near, True)
    dg.opp_half(1)
    dg.onear_a()
    dg.far_step()
    add_grad([dg.opp, dg.far[0]])
    dg.onear_b()
    dg.onear_rest()
    add_grad(dg.onear)
    lax.fori_loop(1, 16, loss_got, 0)
    loss_sum = l_r[0]
    for i in range(1, 16):
        loss_sum = loss_sum + l_r[i]
    out_l[...] = loss_sum / DS
    dg.ofar_step()
    add_grad([dg.far[1]])
    send(g_acc.at[1 - c], g_in, x_ss.at[7], x_rs.at[7], sib)
    arrive(g_in, x_ss.at[7], x_rs.at[7])
    out_g[...] = (g_acc[c] + g_in[...]).astype(BF16)

    flush()
    lax.fori_loop(1, 16, loss_end, 0)


def reduce_buffers():
    block = (ROWS, COLS)
    return [
        pltpu.VMEM((2, 64, COLS), BF16),
        pltpu.VMEM((2, 64, COLS), BF16),
        pltpu.VMEM((2,) + block, BF16),
        pltpu.VMEM((2,) + block, BF16),
        pltpu.VMEM((2,) + block, BF16),
        pltpu.VMEM((2,) + block, BF16),
        pltpu.VMEM(block, BF16),
        pltpu.VMEM(block, BF16),
        pltpu.VMEM(block, F32),
    ]


def on_device(
    teacher_hidden, teacher_gain, projector, student_hidden, student_gain,
    query_weight, kv_weight, out_weight, doc_ids,
):
    block = (ROWS, COLS)
    hbm = pl.BlockSpec(memory_space=pltpu.HBM)
    vmem = pl.BlockSpec(memory_space=pltpu.VMEM)
    dma = pltpu.SemaphoreType.DMA
    out_s, out_l, out_g = pl.pallas_call(
        body,
        out_shape=(
            jax.ShapeDtypeStruct(block, BF16),
            jax.ShapeDtypeStruct((1, ROWS), F32),
            jax.ShapeDtypeStruct((ROWS, 256), BF16),
        ),
        in_specs=[hbm] * 9,
        out_specs=(vmem, vmem, vmem),
        scratch_shapes=[
            pltpu.VMEM((1, 1024), F32),
            pltpu.VMEM((1, COLS), F32),
            pltpu.VMEM((1, ROWS), jnp.int32),
            pltpu.VMEM((ROWS, 1024), BF16),
            pltpu.VMEM((8, ROWS, 1024), BF16),
            pltpu.VMEM((2, 1024, COLS), BF16),
            pltpu.VMEM((8, 2, COLS, 256), BF16),
            pltpu.VMEM((8, 2, 2, 32, COLS), BF16),
            pltpu.VMEM((8, 2, 256, COLS), BF16),
            pltpu.VMEM((64, ROWS), F32),
            pltpu.VMEM((64, ROWS), F32),
            pltpu.VMEM((8,) + block, BF16),
            pltpu.VMEM((1, 768), F32),
            pltpu.VMEM((8, 1, 768), F32),
            pltpu.VMEM((1, 256), F32),
            pltpu.VMEM((1, 256), F32),
            pltpu.VMEM((ROWS, 128), F32),
            pltpu.VMEM((2, ROWS, 256), F32),
            pltpu.VMEM((ROWS, 256), F32),
            pltpu.VMEM((2, 64, ROWS), F32),
            pltpu.VMEM((64, ROWS), F32),
            pltpu.VMEM((4, 16, ROWS), BF16),
            pltpu.VMEM((16, 16, ROWS), BF16),
            pltpu.VMEM((2, ROWS, HEAD_DIM), BF16),
            pltpu.VMEM((2, BACK + 1, ROWS, HEAD_DIM), BF16),
            pltpu.VMEM((8, 1, ROWS), jnp.int32),
            pltpu.VMEM((8, 1, ROWS), jnp.int32),
            pltpu.VMEM((2, ROWS, HEAD_DIM), BF16),
            pltpu.VMEM((4, ROWS, HEAD_DIM), BF16),
            pltpu.VMEM((ROWS, (BACK + 1) * ROWS), F32),
            pltpu.VMEM((8,) + block, F32),
            pltpu.VMEM((4,) + block, F32),
            pltpu.VMEM((8,) + block, F32),
            pltpu.VMEM((2,) + block, BF16),
            pltpu.VMEM((8,) + block, BF16),
            pltpu.VMEM((8,) + block, BF16),
            pltpu.VMEM((2,) + block, BF16),
            *reduce_buffers(),
            *reduce_buffers(),
            pltpu.VMEM(block, BF16),
            pltpu.VMEM(block, BF16),
            pltpu.VMEM((ROWS, 128), F32),
            pltpu.VMEM((8,) + block, BF16),
            pltpu.VMEM((2, ROWS, 256), F32),
            pltpu.VMEM((ROWS, 256), F32),
            pltpu.VMEM((ROWS, 128), F32),
            pltpu.VMEM((1, ROWS), F32),
            pltpu.VMEM((16, 1, ROWS), F32),
            dma((10,)),
            *[dma((8,)) for _ in range(10)],
            dma((16,)), dma((16,)), dma((8,)), dma((8,)),
            dma((24,)), dma((24,)), dma((24,)), dma((24,)),
            dma((16,)), dma((16,)), dma((16,)), dma((16,)),
            dma((9,)), dma((9,)), dma((9,)), dma((9,)), dma((9,)), dma((9,)),
            dma((24,)), dma((24,)), dma((24,)), dma((24,)),
            dma((2,)), dma((2,)),
            dma((16,)), dma((16,)),
        ],
        compiler_params=pltpu.CompilerParams(
            collective_id=0, has_side_effects=True, vmem_limit_bytes=40 * 1024 * 1024
        ),
    )(
        *(
            pltpu.with_memory_space_constraint(one, pltpu.HBM)
            for one in (
                teacher_hidden, teacher_gain.reshape(1, -1), projector, student_hidden,
                student_gain.reshape(1, -1), query_weight.reshape(8, 2, COLS, 256), jnp.transpose(kv_weight, (0, 2, 1)),
                out_weight, doc_ids.reshape(1, -1),
            )
        )
    )
    return out_s, out_l.reshape(ROWS), out_g


def solution(mesh):
    in_specs = (
        P("seq", "tensor"),
        P("tensor"),
        P("tensor", "seq"),
        P("seq", "tensor"),
        P("tensor"),
        P(None, "tensor"),
        P(None, None, "tensor"),
        P("tensor", None),
        P("seq"),
    )
    out_specs = (P("seq", "tensor"), P("seq"), P("seq", "tensor"))
    return jax.shard_map(
        on_device, mesh=mesh, in_specs=in_specs, out_specs=out_specs, check_vma=False
    )
```

profile of v0, /device:TPU:1, one launch (start us, length us, event | category | flops | bytes accessed | tf_op | source)
XLA Modules:
  0.0 92.7 jit_solution(8174836143537528051)
XLA Ops:
  0.6 90.2 %shard_map.112 = (bf16[128,512]{1,0:T(8,128)(2,1)S(1)}, f32[1,128]{1,0:T(1,128)S(1)}, bf16[128,256]{1,0:T(8,128)(2,1)S(1)}) custom-call(bf16[128,1024]{1,0:T(8,128)(2,1)} %th_h.1, f32[1,1024]{1,0:T(1,128)} %bitcast.9, bf16[1024,512]{1,0:T(8,128)(2,1)} %pj_h.1, bf16[128,512]{1,0:T(8,128)(2,1)} %sh_h.1, f32[1,512]{1,0:T(1,128)} %bitcast.10, ...), custom_call_target="tpu_custom_call" | custom-call | tf_op jit(solution)/shard_map/pallas_call | solution.py:791
  90.9 0.7 copy.15
  91.5 0.5 copy.16
  92.0 0.6 copy.17
where the time goes:
time: 92.8 us; the launch traced here: 92.7 us
  Pallas kernels  90.2 us (97%)
  local copies, waits for them, and re-layouts  1.8 us (2%)
    pallas_call x1, Pallas kernels, on_device(): pl.pallas_call(body, out_shape=(jax.ShapeDtypeStruct(block, BF16), jax.Sh...  90.2 us

commit v1 on v0

--- a/solution.py
+++ b/solution.py
@@ -126,6 +126,9 @@
         wo_send(j).wait_send()
         return carry
 
+    lax.fori_loop(0, 8, wkv_go, 0)
+    l_wq = load(wq_h.at[:, c], wq.at[:, c], 3)
+
     kv_r[...] = jnp.zeros(kv_r.shape, BF16)
 
     barrier = pltpu.get_barrier_semaphore()
@@ -192,7 +195,7 @@
             self.got_half(self.far[1], 1, 13)
 
     def pj_send(k):
-        rows = pl.ds(k * 128, 128)
+        rows = pl.ds(k * 256, 256)
         send(pj_h.at[rows], pj.at[yl, rows], p_ss.at[k], p_rs.at[k], dev_yl)
 
     def wkv_send(j):
@@ -218,8 +221,6 @@
 
     ag = Gather(hb, ag_ss, ag_rs)
     l_sh.wait()
-    pl.semaphore_wait(barrier, 7)
-    ag.begin(0)
 
     z_slot = 0
     l_th.wait()
@@ -283,18 +284,20 @@
         else:
             send(docs_z, docs_o, dc_ss.at[8], dc_rs.at[8], dev_yl)
 
+    pl.semaphore_wait(barrier, 7)
     small_send(0, 0, dev_yo)
     small_send(0, 1, dev_xp)
     small_send(0, 2, dev_xm)
+    ag.begin(0)
     ag.begin(1)
     docs_send(0, 0, dev_zp)
     docs_send(0, 4, dev_zm)
     z_send(0)
     pj_send(0)
-    lax.fori_loop(0, 8, wkv_go, 0)
-    l_wq = load(wq_h.at[:, c], wq.at[:, c], 3)
     lax.fori_loop(0, 8, w_go, 0)
     z_send(1)
+    pj_send(1)
+    pj_send(2)
     l_pj = load(pj_h, pj.at[yl], 4)
 
     entry = lax.broadcasted_iota(jnp.int32, (64, ROWS), 0).astype(F32)
@@ -332,7 +335,6 @@
     small_send(3, 5, dev_xm)
     docs_step(0)
     ag.near_relay()
-    pj_send(1)
     small_got(6, 3)
     docs_step(1)
     small_got(4, 4)
@@ -341,7 +343,7 @@
     ag.near_rest()
     ag.opp_half(0)
     z_step(0)
-    pj_send(2)
+    pj_send(3)
     small_got(7, 6)
     sums = sg_r[0][:, COLS:COLS + 256]
     for i in range(1, 8):
@@ -350,7 +352,6 @@
     send(sum_s, sum_r, x_ss.at[2], x_rs.at[2], sib)
     docs_step(2)
     ag.opp_half(1)
-    pj_send(3)
     arrive(sum_r, x_ss.at[2], x_rs.at[2])
     sums = sum_s[...] + sum_r[...]
     ts_v[...] = jnp.broadcast_to(lax.rsqrt(sums[:, 0:128] / DT + 1e-05), (ROWS, 128)).T
@@ -358,18 +359,14 @@
     docs_step(3)
     z_step(1)
     ag.onear_a()
-    pj_send(4)
     l_wq.wait()
     process([mine] + ag.near, True)
     ag.onear_b()
-    pj_send(5)
     z_step(2)
     ag.far_step()
     process([ag.opp, ag.far[0]])
-    pj_send(6)
     ag.onear_rest()
     process(ag.onear)
-    pj_send(7)
     z_step(3)
     ag.ofar_step()
     process([ag.far[1]])
@@ -402,6 +399,8 @@
         return carry
 
     lax.fori_loop(1, 16, kvx_go, 0)
+    lax.fori_loop(0, 8, wo_fetch, 0)
+    lax.fori_loop(0, 8, wo_go, 0)
     z_step(4)
 
     cos2 = jnp.concatenate([cos_t[...], cos_t[...]], axis=0).T
@@ -590,13 +589,10 @@
     t_own[first] = products(c, yl, 0, 1024)
     rt.far(0)
     rt.near(0)
-    lax.fori_loop(0, 8, wo_fetch, 0)
-    lax.fori_loop(0, 8, wo_go, 0)
 
     other = pl.ds((1 - yl) * 4, 4)
     for k in range(4):
-        for part in (2 * k, 2 * k + 1):
-            arrive(pj.at[1 - yl, pl.ds(part * 128, 128)], p_ss.at[part], p_rs.at[part])
+        arrive(pj.at[1 - yl, pl.ds(k * 256, 256)], p_ss.at[k], p_rs.at[k])
         theirs = products(1 - c, 1 - yl, k, 256)
         if k == 0:
             t_part[...] = theirs
@@ -615,11 +611,9 @@
     rt.far(1)
     rt.near(1)
     rt.join_one(0)
-    for k in (1, 2, 3, 4):
+    for k in range(1, BACK + 1):
         kv_mid(k)
     rt.relay(1)
-    for k in (5, 6, 7, 8):
-        kv_mid(k)
 
     lax.fori_loop(1, BACK + 1, kv_got, 0)
     keys = jnp.concatenate([kv_r[0, j] for j in range(BACK + 1)], axis=1)
@@ -646,10 +640,10 @@
 
     out_block(0, 0)
     ro.far(0)
-    rt.join_one(1)
     out_block(1, 0)
     out_block(2, 0)
     ro.near(0)
+    rt.join_one(1)
     out_block(0, 1)
     ro.relay(0)
     ro.far(1)
@@ -679,8 +673,12 @@
     ro.join_other()
     ro.join_mine()
 
+    early = list(started)
+    started.clear()
+
     def before_end():
-        flush()
+        for one in early:
+            one.wait_send()
         lax.fori_loop(0, 8, w_end, 0)
         lax.fori_loop(0, 8, wo_end, 0)
         lax.fori_loop(1, 16, kvx_end, 0)

time: 92.8 us -> 90.4 us (0.974)
  Pallas kernels: 90.2 us -> 87.9 us
    pallas_call x1, Pallas kernels: 90.2 us -> 87.9 us  [on_device(): pl.pallas_call(body, out_shape=(jax.ShapeDtypeStruct(block, BF16), jax.Sh...]
where the time goes in v1:
time: 90.4 us; the launch traced here: 90.3 us
  Pallas kernels  87.9 us (97%)
  local copies, waits for them, and re-layouts  1.8 us (2%)
    pallas_call x1, Pallas kernels, on_device(): pl.pallas_call(body, out_shape=(jax.ShapeDtypeStruct(block, BF16), jax.Sh...  87.9 us

profile of v1, /device:TPU:1, one launch (start us, length us, event | category | flops | bytes accessed | tf_op | source)
XLA Modules:
  0.0 90.3 jit_solution(4915949254736598276)
XLA Ops:
  0.6 87.9 %shard_map.112 = (bf16[128,512]{1,0:T(8,128)(2,1)S(1)}, f32[1,128]{1,0:T(1,128)S(1)}, bf16[128,256]{1,0:T(8,128)(2,1)S(1)}) custom-call(bf16[128,1024]{1,0:T(8,128)(2,1)} %th_h.1, f32[1,1024]{1,0:T(1,128)} %bitcast.9, bf16[1024,512]{1,0:T(8,128)(2,1)} %pj_h.1, bf16[128,512]{1,0:T(8,128)(2,1)} %sh_h.1, f32[1,512]{1,0:T(1,128)} %bitcast.10, ...), custom_call_target="tpu_custom_call" | custom-call | tf_op jit(solution)/shard_map/pallas_call | solution.py:789
  88.5 0.7 copy.15
  89.2 0.5 copy.16
  89.7 0.6 copy.17

commit v2 on v1

--- a/solution.py
+++ b/solution.py
@@ -292,12 +292,11 @@
     ag.begin(1)
     docs_send(0, 0, dev_zp)
     docs_send(0, 4, dev_zm)
+    pj_send(0)
     z_send(0)
-    pj_send(0)
+    pj_send(1)
+    z_send(1)
     lax.fori_loop(0, 8, w_go, 0)
-    z_send(1)
-    pj_send(1)
-    pj_send(2)
     l_pj = load(pj_h, pj.at[yl], 4)
 
     entry = lax.broadcasted_iota(jnp.int32, (64, ROWS), 0).astype(F32)
@@ -341,6 +340,7 @@
     small_send(4, 6, dev_xp)
     small_got(5, 5)
     ag.near_rest()
+    pj_send(2)
     ag.opp_half(0)
     z_step(0)
     pj_send(3)
@@ -611,9 +611,12 @@
     rt.far(1)
     rt.near(1)
     rt.join_one(0)
-    for k in range(1, BACK + 1):
+    for k in (1, 2, 3, 4):
         kv_mid(k)
     rt.relay(1)
+    for k in (5, 6, 7, 8):
+        kv_mid(k)
+    rt.join_one(1)
 
     lax.fori_loop(1, BACK + 1, kv_got, 0)
     keys = jnp.concatenate([kv_r[0, j] for j in range(BACK + 1)], axis=1)
@@ -638,37 +641,38 @@
         slot = ro.slot(k, i)
         o_own[slot] = jnp.dot(attn, wo[slot].reshape(COLS, COLS), preferred_element_type=F32)
 
+    def t3(h):
+        at = pl.ds(h * 64, 64)
+        return copy(t3_s.at[at], t3_r.at[at], t3_ss.at[h], t3_rs.at[h], dev_t3)
+
+    def t3_go(h):
+        rows = slice(h * 64, h * 64 + 64)
+        t3_s[rows] = rt.last(h).astype(BF16)
+
+        @pl.when(stays)
+        def _():
+            t3_r[rows] = t3_s[rows]
+
+        @pl.when(jnp.logical_not(stays))
+        def _():
+            t3(h).start()
+
     out_block(0, 0)
     ro.far(0)
     out_block(1, 0)
     out_block(2, 0)
     ro.near(0)
-    rt.join_one(1)
     out_block(0, 1)
     ro.relay(0)
     ro.far(1)
+    t3_go(0)
     out_block(1, 1)
     out_block(2, 1)
     ro.near(1)
+    t3_go(1)
     out_block(3, 0)
     out_block(3, 1)
     ro.relay(1)
-
-    def t3(h):
-        at = pl.ds(h * 64, 64)
-        return copy(t3_s.at[at], t3_r.at[at], t3_ss.at[h], t3_rs.at[h], dev_t3)
-
-    for h in range(2):
-        rows = slice(h * 64, h * 64 + 64)
-        t3_s[rows] = rt.last(h).astype(BF16)
-
-        @pl.when(stays)
-        def _():
-            t3_r[rows] = t3_s[rows]
-
-        @pl.when(jnp.logical_not(stays))
-        def _():
-            t3(h).start()
 
     ro.join_other()
     ro.join_mine()

time: 90.4 us -> 93.9 us (1.039)
  Pallas kernels: 87.9 us -> 91.4 us
    pallas_call x1, Pallas kernels: 87.9 us -> 91.4 us  [on_device(): pl.pallas_call(body, out_shape=(jax.ShapeDtypeStruct(block, BF16), jax.Sh...]
where the time goes in v2:
time: 93.9 us; the launch traced here: 93.8 us
  Pallas kernels  91.4 us (97%)
  local copies, waits for them, and re-layouts  1.8 us (2%)
    pallas_call x1, Pallas kernels, on_device(): pl.pallas_call(body, out_shape=(jax.ShapeDtypeStruct(block, BF16), jax.Sh...  91.4 us

profile of v2, /device:TPU:1, one launch (start us, length us, event | category | flops | bytes accessed | tf_op | source)
XLA Modules:
  0.0 93.8 jit_solution(4518030783424988782)
XLA Ops:
  0.6 91.4 %shard_map.112 = (bf16[128,512]{1,0:T(8,128)(2,1)S(1)}, f32[1,128]{1,0:T(1,128)S(1)}, bf16[128,256]{1,0:T(8,128)(2,1)S(1)}) custom-call(bf16[128,1024]{1,0:T(8,128)(2,1)} %th_h.1, f32[1,1024]{1,0:T(1,128)} %bitcast.9, bf16[1024,512]{1,0:T(8,128)(2,1)} %pj_h.1, bf16[128,512]{1,0:T(8,128)(2,1)} %sh_h.1, f32[1,512]{1,0:T(1,128)} %bitcast.10, ...), custom_call_target="tpu_custom_call" | custom-call | tf_op jit(solution)/shard_map/pallas_call | solution.py:793
  92.0 0.7 copy.15
  92.7 0.5 copy.16
  93.2 0.6 copy.17

commit v3 on v1

--- a/solution.py
+++ b/solution.py
@@ -31,7 +31,7 @@
     tgain, sgain, docs, th_v, tg, pj, wq, wkv, wo, cos_t, sin_t,
     hb, sg_s, sg_r, sum_s, sum_r, scale_v, q_acc, q_in, kv_acc, kv_in,
     kvx_s, kvx_r, kv_own, kv_r, docs_z, docs_o, q_v, attn_v, bias,
-    t_own, t_part, o_own, o_x2, t_sib_s, t_sib_r, t_x2, t_ra, t_rb, t_xp, t_xm, t_fm, t_fp, t_ys, t_yr, t_fin,
+    t_own, t_part, o_own, o_x2, t_sib_s, t_sib_r, t_x2, t_ra, t_rb, t_xp, t_xm, t_fm, t_fp,
     o_ra, o_rb, o_xp, o_xm, o_fm, o_fp, o_ys, o_yr, o_fin,
     t3_s, t3_r, ts_v, db, g_acc, g_in, l_v, l_s, l_r,
     load_sem, w_load, w_ss, w_rs, v_load, v_ss, v_rs, u_ss, u_rs, x_ss, x_rs, z_ss, z_rs, p_ss, p_rs,
@@ -57,7 +57,6 @@
     dev_zm = (yl * 8 + (z + 7) % 8, t)
     dev_yl = ((1 - yl) * 8 + z, t)
     turn = jnp.where(c == 0, x, jnp.where(x == 0, 4, 8 - x))
-    dev_t3 = (yl * 8 + (z + turn) % 8, yh * 8 + z)
     stays = (z == 0) & (x == 0) & (c == 0)
 
     started = []
@@ -535,21 +534,6 @@
             self.got(self.fp.at[i, at], (14, 18)[h] + i)
             return self.pair(3, i, h) + self.fm[i, rows].astype(F32) + self.fp[i, rows].astype(F32)
 
-        def join_one(self, i):
-            mine = self.y_order[i] == yh
-            for h in range(2):
-                rows = slice(h * 64, h * 64 + 64)
-                value = self.join(i, h)
-
-                @pl.when(mine)
-                def _():
-                    self.fin[rows] = value
-
-                @pl.when(jnp.logical_not(mine))
-                def _():
-                    self.ys[rows] = value.astype(BF16)
-                    self.to_opp(h).start()
-
         def to_opp(self, h):
             at = pl.ds(h * 64, 64)
             return copy(self.ys.at[at], self.yr.at[at], self.ss.at[20 + h], self.rs.at[20 + h], dev_yo)
@@ -572,7 +556,28 @@
             self.got(self.yr.at[pl.ds(h * 64, 64)], 20 + h)
             return self.fin[rows] + self.yr[rows].astype(F32)
 
-    rt = Reduce((yl, 1 - yl), t_own, t_sib_s, t_sib_r, t_x2, t_ra, t_rb, t_xp, t_xm, t_fm, t_fp, t_ys, t_yr, t_fin, t_ss, t_rs)
+    rt = Reduce((yl, 1 - yl), t_own, t_sib_s, t_sib_r, t_x2, t_ra, t_rb, t_xp, t_xm, t_fm, t_fp, None, None, None, t_ss, t_rs)
+
+    def t3(i, h):
+        at = pl.ds(h * 64, 64)
+        dev = (yl * 8 + (z + turn) % 8, rt.y_order[i] * 8 + z)
+        return copy(t3_s.at[i, at], t3_r.at[yh, at], t3_ss.at[i * 2 + h], t3_rs.at[yh * 2 + h], dev)
+
+    def t3_stays(i):
+        return stays & (rt.y_order[i] == yh)
+
+    def t_place(i):
+        for h in range(2):
+            rows = slice(h * 64, h * 64 + 64)
+            t3_s[i, rows] = rt.join(i, h).astype(BF16)
+
+            @pl.when(t3_stays(i))
+            def _():
+                t3_r[yh, rows] = t3_s[i, rows]
+
+            @pl.when(jnp.logical_not(t3_stays(i)))
+            def _():
+                t3(i, h).start()
 
     z_step(5)
     z_step(6)
@@ -610,7 +615,7 @@
             rt.relay(0)
     rt.far(1)
     rt.near(1)
-    rt.join_one(0)
+    t_place(0)
     for k in range(1, BACK + 1):
         kv_mid(k)
     rt.relay(1)
@@ -643,7 +648,7 @@
     out_block(1, 0)
     out_block(2, 0)
     ro.near(0)
-    rt.join_one(1)
+    t_place(1)
     out_block(0, 1)
     ro.relay(0)
     ro.far(1)
@@ -654,22 +659,6 @@
     out_block(3, 1)
     ro.relay(1)
 
-    def t3(h):
-        at = pl.ds(h * 64, 64)
-        return copy(t3_s.at[at], t3_r.at[at], t3_ss.at[h], t3_rs.at[h], dev_t3)
-
-    for h in range(2):
-        rows = slice(h * 64, h * 64 + 64)
-        t3_s[rows] = rt.last(h).astype(BF16)
-
-        @pl.when(stays)
-        def _():
-            t3_r[rows] = t3_s[rows]
-
-        @pl.when(jnp.logical_not(stays))
-        def _():
-            t3(h).start()
-
     ro.join_other()
     ro.join_mine()
 
@@ -683,13 +672,13 @@
         lax.fori_loop(0, 8, wo_end, 0)
         lax.fori_loop(1, 16, kvx_end, 0)
         lax.fori_loop(1, BACK + 1, kv_end, 0)
-        rt.end()
         ro.end()
-
-        @pl.when(jnp.logical_not(stays))
-        def _():
-            t3(0).wait_send()
-            t3(1).wait_send()
+        for i in range(2):
+
+            @pl.when(jnp.logical_not(t3_stays(i)))
+            def _():
+                t3(i, 0).wait_send()
+                t3(i, 1).wait_send()
 
     dg = Gather(db, dg_ss, dg_rs)
     for h in range(2):
@@ -697,11 +686,14 @@
         mixed = hb[mine, rows].astype(F32) + ro.last(h)
         out_s[rows] = mixed.astype(BF16)
 
-        @pl.when(jnp.logical_not(stays))
-        def _():
-            arrive(t3_r.at[pl.ds(h * 64, 64)], t3_ss.at[h], t3_rs.at[h])
-
-        target = t3_r[rows].astype(F32) * jnp.concatenate([ts_v[rows]] * 4, axis=1)
+        for p in range(2):
+
+            @pl.when(jnp.logical_not(stays & (yh == p)))
+            def _():
+                arrive(t3_r.at[p, pl.ds(h * 64, 64)], t3_ss.at[h], t3_rs.at[p * 2 + h])
+
+        target = t3_r[0, rows].astype(F32) + t3_r[1, rows].astype(F32)
+        target = target * jnp.concatenate([ts_v[rows]] * 4, axis=1)
         difference = mixed - target
         db[mine, rows] = difference.astype(BF16)
         dg.begin(h)
@@ -833,10 +825,10 @@
             pltpu.VMEM((8,) + block, BF16),
             pltpu.VMEM((8,) + block, BF16),
             pltpu.VMEM((2,) + block, BF16),
+            *reduce_buffers()[:6],
             *reduce_buffers(),
-            *reduce_buffers(),
-            pltpu.VMEM(block, BF16),
-            pltpu.VMEM(block, BF16),
+            pltpu.VMEM((2,) + block, BF16),
+            pltpu.VMEM((2,) + block, BF16),
             pltpu.VMEM((ROWS, 128), F32),
             pltpu.VMEM((8,) + block, BF16),
             pltpu.VMEM((2, ROWS, 256), F32),
@@ -851,7 +843,7 @@
             dma((16,)), dma((16,)), dma((16,)), dma((16,)),
             dma((9,)), dma((9,)), dma((9,)), dma((9,)), dma((9,)), dma((9,)),
             dma((24,)), dma((24,)), dma((24,)), dma((24,)),
-            dma((2,)), dma((2,)),
+            dma((4,)), dma((4,)),
             dma((16,)), dma((16,)),
         ],
         compiler_params=pltpu.CompilerParams(

time: 90.4 us -> 89.8 us (level)
  no operation moved by 1% of the time
where the time goes in v3:
time: 89.8 us; the launch traced here: 89.7 us
  Pallas kernels  87.3 us (97%)
  local copies, waits for them, and re-layouts  1.8 us (2%)
    pallas_call x1, Pallas kernels, on_device(): pl.pallas_call(body, out_shape=(jax.ShapeDtypeStruct(block, BF16), jax.Sh...  87.3 us
    unnamed x3, local copies, waits for them, and re-layouts  1.8 us

profile of v3, /device:TPU:1, one launch (start us, length us, event | category | flops | bytes accessed | tf_op | source)
XLA Modules:
  0.0 89.7 jit_solution(14436914929608170857)
XLA Ops:
  0.6 87.3 %shard_map.112 = (bf16[128,512]{1,0:T(8,128)(2,1)S(1)}, f32[1,128]{1,0:T(1,128)S(1)}, bf16[128,256]{1,0:T(8,128)(2,1)S(1)}) custom-call(bf16[128,1024]{1,0:T(8,128)(2,1)} %th_h.1, f32[1,1024]{1,0:T(1,128)} %bitcast.9, bf16[1024,512]{1,0:T(8,128)(2,1)} %pj_h.1, bf16[128,512]{1,0:T(8,128)(2,1)} %sh_h.1, f32[1,512]{1,0:T(1,128)} %bitcast.10, ...), custom_call_target="tpu_custom_call" | custom-call | tf_op jit(solution)/shard_map/pallas_call | solution.py:781
  87.9 0.7 copy.15
  88.6 0.5 copy.16
  89.1 0.6 copy.17

commit v4 on v3

--- a/solution.py
+++ b/solution.py
@@ -194,7 +194,7 @@
             self.got_half(self.far[1], 1, 13)
 
     def pj_send(k):
-        rows = pl.ds(k * 256, 256)
+        rows = pl.ds(k * 128, 128)
         send(pj_h.at[rows], pj.at[yl, rows], p_ss.at[k], p_rs.at[k], dev_yl)
 
     def wkv_send(j):
@@ -220,6 +220,8 @@
 
     ag = Gather(hb, ag_ss, ag_rs)
     l_sh.wait()
+    pl.semaphore_wait(barrier, 7)
+    ag.begin(0)
 
     z_slot = 0
     l_th.wait()
@@ -283,11 +285,9 @@
         else:
             send(docs_z, docs_o, dc_ss.at[8], dc_rs.at[8], dev_yl)
 
-    pl.semaphore_wait(barrier, 7)
     small_send(0, 0, dev_yo)
     small_send(0, 1, dev_xp)
     small_send(0, 2, dev_xm)
-    ag.begin(0)
     ag.begin(1)
     docs_send(0, 0, dev_zp)
     docs_send(0, 4, dev_zm)
@@ -295,8 +295,6 @@
     pj_send(0)
     lax.fori_loop(0, 8, w_go, 0)
     z_send(1)
-    pj_send(1)
-    pj_send(2)
     l_pj = load(pj_h, pj.at[yl], 4)
 
     entry = lax.broadcasted_iota(jnp.int32, (64, ROWS), 0).astype(F32)
@@ -334,6 +332,7 @@
     small_send(3, 5, dev_xm)
     docs_step(0)
     ag.near_relay()
+    pj_send(1)
     small_got(6, 3)
     docs_step(1)
     small_got(4, 4)
@@ -342,7 +341,7 @@
     ag.near_rest()
     ag.opp_half(0)
     z_step(0)
-    pj_send(3)
+    pj_send(2)
     small_got(7, 6)
     sums = sg_r[0][:, COLS:COLS + 256]
     for i in range(1, 8):
@@ -351,6 +350,7 @@
     send(sum_s, sum_r, x_ss.at[2], x_rs.at[2], sib)
     docs_step(2)
     ag.opp_half(1)
+    pj_send(3)
     arrive(sum_r, x_ss.at[2], x_rs.at[2])
     sums = sum_s[...] + sum_r[...]
     ts_v[...] = jnp.broadcast_to(lax.rsqrt(sums[:, 0:128] / DT + 1e-05), (ROWS, 128)).T
@@ -358,14 +358,18 @@
     docs_step(3)
     z_step(1)
     ag.onear_a()
+    pj_send(4)
     l_wq.wait()
     process([mine] + ag.near, True)
     ag.onear_b()
+    pj_send(5)
     z_step(2)
     ag.far_step()
     process([ag.opp, ag.far[0]])
+    pj_send(6)
     ag.onear_rest()
     process(ag.onear)
+    pj_send(7)
     z_step(3)
     ag.ofar_step()
     process([ag.far[1]])
@@ -597,7 +601,8 @@
 
     other = pl.ds((1 - yl) * 4, 4)
     for k in range(4):
-        arrive(pj.at[1 - yl, pl.ds(k * 256, 256)], p_ss.at[k], p_rs.at[k])
+        for piece in (2 * k, 2 * k + 1):
+            arrive(pj.at[1 - yl, pl.ds(piece * 128, 128)], p_ss.at[piece], p_rs.at[piece])
         theirs = products(1 - c, 1 - yl, k, 256)
         if k == 0:
             t_part[...] = theirs
@@ -618,7 +623,6 @@
     t_place(0)
     for k in range(1, BACK + 1):
         kv_mid(k)
-    rt.relay(1)
 
     lax.fori_loop(1, BACK + 1, kv_got, 0)
     keys = jnp.concatenate([kv_r[0, j] for j in range(BACK + 1)], axis=1)
@@ -632,6 +636,7 @@
         attn_v[c * 2 + h] = (acc / total).astype(BF16)
         send(attn_v.at[c * 2 + h], attn_v.at[c * 2 + h], x_ss.at[5 + h], x_rs.at[5 + h], sib)
     lax.fori_loop(0, 8, wo_got, 0)
+    rt.relay(1)
 
     ro = Reduce((yo_, yh), o_own, None, None, o_x2, o_ra, o_rb, o_xp, o_xm, o_fm, o_fp, o_ys, o_yr, o_fin, o_ss, o_rs)
 
@@ -648,13 +653,13 @@
     out_block(1, 0)
     out_block(2, 0)
     ro.near(0)
-    t_place(1)
     out_block(0, 1)
     ro.relay(0)
     ro.far(1)
     out_block(1, 1)
     out_block(2, 1)
     ro.near(1)
+    t_place(1)
     out_block(3, 0)
     out_block(3, 1)
     ro.relay(1)

time: 89.8 us -> 90.4 us (level)
  no operation moved by 1% of the time
where the time goes in v4:
time: 90.4 us; the launch traced here: 90.3 us
  Pallas kernels  87.8 us (97%)
  local copies, waits for them, and re-layouts  1.8 us (2%)
    pallas_call x1, Pallas kernels, on_device(): pl.pallas_call(body, out_shape=(jax.ShapeDtypeStruct(block, BF16), jax.Sh...  87.8 us

profile of v4, /device:TPU:1, one launch (start us, length us, event | category | flops | bytes accessed | tf_op | source)
XLA Modules:
  0.0 90.3 jit_solution(9500321224920082462)
XLA Ops:
  0.6 87.8 %shard_map.112 = (bf16[128,512]{1,0:T(8,128)(2,1)S(1)}, f32[1,128]{1,0:T(1,128)S(1)}, bf16[128,256]{1,0:T(8,128)(2,1)S(1)}) custom-call(bf16[128,1024]{1,0:T(8,128)(2,1)} %th_h.1, f32[1,1024]{1,0:T(1,128)} %bitcast.9, bf16[1024,512]{1,0:T(8,128)(2,1)} %pj_h.1, bf16[128,512]{1,0:T(8,128)(2,1)} %sh_h.1, f32[1,512]{1,0:T(1,128)} %bitcast.10, ...), custom_call_target="tpu_custom_call" | custom-call | tf_op jit(solution)/shard_map/pallas_call | solution.py:786
  88.5 0.7 copy.15
  89.1 0.5 copy.16
  89.6 0.6 copy.17

commit v5 on v3

--- a/solution.py
+++ b/solution.py
@@ -616,9 +616,12 @@
     rt.far(1)
     rt.near(1)
     t_place(0)
-    for k in range(1, BACK + 1):
+    for k in (1, 2, 3, 4):
         kv_mid(k)
     rt.relay(1)
+    for k in (5, 6, 7, 8):
+        kv_mid(k)
+    t_place(1)
 
     lax.fori_loop(1, BACK + 1, kv_got, 0)
     keys = jnp.concatenate([kv_r[0, j] for j in range(BACK + 1)], axis=1)
@@ -648,7 +651,6 @@
     out_block(1, 0)
     out_block(2, 0)
     ro.near(0)
-    t_place(1)
     out_block(0, 1)
     ro.relay(0)
     ro.far(1)

time: 89.8 us -> 93.5 us (1.041)
  Pallas kernels: 87.3 us -> 91 us
    pallas_call x1, Pallas kernels: 87.3 us -> 91 us  [on_device(): pl.pallas_call(body, out_shape=(jax.ShapeDtypeStruct(block, BF16), jax.Sh...]
where the time goes in v5:
time: 93.5 us; the launch traced here: 93.4 us
  Pallas kernels  91 us (97%)
  local copies, waits for them, and re-layouts  1.8 us (2%)
    pallas_call x1, Pallas kernels, on_device(): pl.pallas_call(body, out_shape=(jax.ShapeDtypeStruct(block, BF16), jax.Sh...  91 us

profile of v5, /device:TPU:1, one launch (start us, length us, event | category | flops | bytes accessed | tf_op | source)
XLA Modules:
  0.0 93.4 jit_solution(413634535130684030)
XLA Ops:
  0.6 91.0 %shard_map.112 = (bf16[128,512]{1,0:T(8,128)(2,1)S(1)}, f32[1,128]{1,0:T(1,128)S(1)}, bf16[128,256]{1,0:T(8,128)(2,1)S(1)}) custom-call(bf16[128,1024]{1,0:T(8,128)(2,1)} %th_h.1, f32[1,1024]{1,0:T(1,128)} %bitcast.9, bf16[1024,512]{1,0:T(8,128)(2,1)} %pj_h.1, bf16[128,512]{1,0:T(8,128)(2,1)} %sh_h.1, f32[1,512]{1,0:T(1,128)} %bitcast.10, ...), custom_call_target="tpu_custom_call" | custom-call | tf_op jit(solution)/shard_map/pallas_call | solution.py:783
  91.6 0.7 copy.15
  92.3 0.5 copy.16
  92.8 0.6 copy.17

commit v6 on v3

--- a/solution.py
+++ b/solution.py
@@ -292,9 +292,9 @@
     docs_send(0, 0, dev_zp)
     docs_send(0, 4, dev_zm)
     z_send(0)
+    z_send(1)
     pj_send(0)
     lax.fori_loop(0, 8, w_go, 0)
-    z_send(1)
     pj_send(1)
     pj_send(2)
     l_pj = load(pj_h, pj.at[yl], 4)
@@ -334,6 +334,7 @@
     small_send(3, 5, dev_xm)
     docs_step(0)
     ag.near_relay()
+    z_step(0)
     small_got(6, 3)
     docs_step(1)
     small_got(4, 4)
@@ -341,7 +342,7 @@
     small_got(5, 5)
     ag.near_rest()
     ag.opp_half(0)
-    z_step(0)
+    z_step(1)
     pj_send(3)
     small_got(7, 6)
     sums = sg_r[0][:, COLS:COLS + 256]
@@ -351,22 +352,22 @@
     send(sum_s, sum_r, x_ss.at[2], x_rs.at[2], sib)
     docs_step(2)
     ag.opp_half(1)
+    z_step(2)
     arrive(sum_r, x_ss.at[2], x_rs.at[2])
     sums = sum_s[...] + sum_r[...]
     ts_v[...] = jnp.broadcast_to(lax.rsqrt(sums[:, 0:128] / DT + 1e-05), (ROWS, 128)).T
     scale_v[...] = jnp.broadcast_to(lax.rsqrt(sums[:, 128:256] / DS + 1e-05), (ROWS, 128)).T
     docs_step(3)
-    z_step(1)
     ag.onear_a()
+    z_step(3)
     l_wq.wait()
     process([mine] + ag.near, True)
     ag.onear_b()
-    z_step(2)
     ag.far_step()
+    z_step(4)
     process([ag.opp, ag.far[0]])
     ag.onear_rest()
     process(ag.onear)
-    z_step(3)
     ag.ofar_step()
     process([ag.far[1]])
     send(kv_acc.at[1 - c], kv_in, x_ss.at[3], x_rs.at[3], sib)
@@ -400,7 +401,6 @@
     lax.fori_loop(1, 16, kvx_go, 0)
     lax.fori_loop(0, 8, wo_fetch, 0)
     lax.fori_loop(0, 8, wo_go, 0)
-    z_step(4)
 
     cos2 = jnp.concatenate([cos_t[...], cos_t[...]], axis=0).T
     sin2 = jnp.concatenate([-sin_t[...], sin_t[...]], axis=0).T

time: 89.8 us -> 90 us (level)
  no operation moved by 1% of the time
where the time goes in v6:
time: 90 us; the launch traced here: 89.9 us
  Pallas kernels  87.5 us (97%)
  local copies, waits for them, and re-layouts  1.8 us (2%)
    pallas_call x1, Pallas kernels, on_device(): pl.pallas_call(body, out_shape=(jax.ShapeDtypeStruct(block, BF16), jax.Sh...  87.5 us

profile of v6, /device:TPU:1, one launch (start us, length us, event | category | flops | bytes accessed | tf_op | source)
XLA Modules:
  0.0 89.9 jit_solution(7216638391742557870)
XLA Ops:
  0.6 87.5 %shard_map.112 = (bf16[128,512]{1,0:T(8,128)(2,1)S(1)}, f32[1,128]{1,0:T(1,128)S(1)}, bf16[128,256]{1,0:T(8,128)(2,1)S(1)}) custom-call(bf16[128,1024]{1,0:T(8,128)(2,1)} %th_h.1, f32[1,1024]{1,0:T(1,128)} %bitcast.9, bf16[1024,512]{1,0:T(8,128)(2,1)} %pj_h.1, bf16[128,512]{1,0:T(8,128)(2,1)} %sh_h.1, f32[1,512]{1,0:T(1,128)} %bitcast.10, ...), custom_call_target="tpu_custom_call" | custom-call | tf_op jit(solution)/shard_map/pallas_call | solution.py:781
  88.1 0.7 copy.15
  88.8 0.5 copy.16
  89.3 0.6 copy.17

commit v7 on v3

--- a/solution.py
+++ b/solution.py
@@ -195,7 +195,12 @@
 
     def pj_send(k):
         rows = pl.ds(k * 256, 256)
-        send(pj_h.at[rows], pj.at[yl, rows], p_ss.at[k], p_rs.at[k], dev_yl)
+        return copy(pj_h.at[rows], pj.at[yl, rows], p_ss.at[k], p_rs.at[k], dev_yl)
+
+    def pj_start(k, half):
+        @pl.when(yl == half)
+        def _():
+            pj_send(k).start()
 
     def wkv_send(j):
         return copy(wkv_part(j, 1 - c), wkv.at[j, c], v_ss.at[j], v_rs.at[j], sib)
@@ -220,6 +225,8 @@
 
     ag = Gather(hb, ag_ss, ag_rs)
     l_sh.wait()
+    pl.semaphore_wait(barrier, 7)
+    ag.begin(0)
 
     z_slot = 0
     l_th.wait()
@@ -283,20 +290,20 @@
         else:
             send(docs_z, docs_o, dc_ss.at[8], dc_rs.at[8], dev_yl)
 
-    pl.semaphore_wait(barrier, 7)
     small_send(0, 0, dev_yo)
     small_send(0, 1, dev_xp)
     small_send(0, 2, dev_xm)
-    ag.begin(0)
     ag.begin(1)
     docs_send(0, 0, dev_zp)
     docs_send(0, 4, dev_zm)
     z_send(0)
-    pj_send(0)
+    pj_start(0, 1)
+    z_send(1)
+    pj_start(1, 1)
     lax.fori_loop(0, 8, w_go, 0)
-    z_send(1)
-    pj_send(1)
-    pj_send(2)
+    pj_start(2, 1)
+    pj_start(3, 1)
+    pj_start(0, 0)
     l_pj = load(pj_h, pj.at[yl], 4)
 
     entry = lax.broadcasted_iota(jnp.int32, (64, ROWS), 0).astype(F32)
@@ -340,9 +347,10 @@
     small_send(4, 6, dev_xp)
     small_got(5, 5)
     ag.near_rest()
+    pj_start(1, 0)
     ag.opp_half(0)
     z_step(0)
-    pj_send(3)
+    pj_start(2, 0)
     small_got(7, 6)
     sums = sg_r[0][:, COLS:COLS + 256]
     for i in range(1, 8):
@@ -351,6 +359,7 @@
     send(sum_s, sum_r, x_ss.at[2], x_rs.at[2], sib)
     docs_step(2)
     ag.opp_half(1)
+    pj_start(3, 0)
     arrive(sum_r, x_ss.at[2], x_rs.at[2])
     sums = sum_s[...] + sum_r[...]
     ts_v[...] = jnp.broadcast_to(lax.rsqrt(sums[:, 0:128] / DT + 1e-05), (ROWS, 128)).T
@@ -618,7 +627,6 @@
     t_place(0)
     for k in range(1, BACK + 1):
         kv_mid(k)
-    rt.relay(1)
 
     lax.fori_loop(1, BACK + 1, kv_got, 0)
     keys = jnp.concatenate([kv_r[0, j] for j in range(BACK + 1)], axis=1)
@@ -632,6 +640,7 @@
         attn_v[c * 2 + h] = (acc / total).astype(BF16)
         send(attn_v.at[c * 2 + h], attn_v.at[c * 2 + h], x_ss.at[5 + h], x_rs.at[5 + h], sib)
     lax.fori_loop(0, 8, wo_got, 0)
+    rt.relay(1)
 
     ro = Reduce((yo_, yh), o_own, None, None, o_x2, o_ra, o_rb, o_xp, o_xm, o_fm, o_fp, o_ys, o_yr, o_fin, o_ss, o_rs)
 
@@ -668,6 +677,8 @@
     def before_end():
         for one in early:
             one.wait_send()
+        for k in range(4):
+            pj_send(k).wait_send()
         lax.fori_loop(0, 8, w_end, 0)
         lax.fori_loop(0, 8, wo_end, 0)
         lax.fori_loop(1, 16, kvx_end, 0)

time: 89.8 us -> 90.2 us (level)
  no operation moved by 1% of the time
where the time goes in v7:
time: 90.2 us; the launch traced here: 90.1 us
  Pallas kernels  87.7 us (97%)
  local copies, waits for them, and re-layouts  1.8 us (2%)
    pallas_call x1, Pallas kernels, on_device(): pl.pallas_call(body, out_shape=(jax.ShapeDtypeStruct(block, BF16), jax.Sh...  87.7 us

profile of v7, /device:TPU:1, one launch (start us, length us, event | category | flops | bytes accessed | tf_op | source)
XLA Modules:
  0.0 90.1 jit_solution(2036924902564036557)
XLA Ops:
  0.6 87.7 %shard_map.112 = (bf16[128,512]{1,0:T(8,128)(2,1)S(1)}, f32[1,128]{1,0:T(1,128)S(1)}, bf16[128,256]{1,0:T(8,128)(2,1)S(1)}) custom-call(bf16[128,1024]{1,0:T(8,128)(2,1)} %th_h.1, f32[1,1024]{1,0:T(1,128)} %bitcast.9, bf16[1024,512]{1,0:T(8,128)(2,1)} %pj_h.1, bf16[128,512]{1,0:T(8,128)(2,1)} %sh_h.1, f32[1,512]{1,0:T(1,128)} %bitcast.10, ...), custom_call_target="tpu_custom_call" | custom-call | tf_op jit(solution)/shard_map/pallas_call | solution.py:792
  88.3 0.7 copy.15
  89.0 0.5 copy.16
  89.5 0.6 copy.17

commit v8 on v3

--- a/solution.py
+++ b/solution.py
@@ -458,7 +458,7 @@
         return carry
 
     arrive(docs_o, dc_ss.at[8], dc_rs.at[8])
-    for k in range(1, BACK + 1):
+    for k in (4, 5, 3, 6, 8, 7, 2, 1):
         kv_go(k)
 
     def docs_back(j):
@@ -731,13 +731,13 @@
     dg.near_relay()
     dg.opp_half(0)
     dg.near_rest()
-    before_end()
     add_grad([mine] + dg.near, True)
     dg.opp_half(1)
     dg.onear_a()
+    dg.onear_b()
     dg.far_step()
     add_grad([dg.opp, dg.far[0]])
-    dg.onear_b()
+    before_end()
     dg.onear_rest()
     add_grad(dg.onear)
     lax.fori_loop(1, 16, loss_got, 0)

time: 89.8 us -> 89.8 us (level)
  no operation moved by 1% of the time
where the time goes in v8:
time: 89.8 us; the launch traced here: 89.7 us
  Pallas kernels  87.3 us (97%)
  local copies, waits for them, and re-layouts  1.8 us (2%)
    pallas_call x1, Pallas kernels, on_device(): pl.pallas_call(body, out_shape=(jax.ShapeDtypeStruct(block, BF16), jax.Sh...  87.3 us
    unnamed x3, local copies, waits for them, and re-layouts  1.8 us

profile of v8, /device:TPU:1, one launch (start us, length us, event | category | flops | bytes accessed | tf_op | source)
XLA Modules:
  0.0 89.7 jit_solution(5227134333040347424)
XLA Ops:
  0.6 87.3 %shard_map.112 = (bf16[128,512]{1,0:T(8,128)(2,1)S(1)}, f32[1,128]{1,0:T(1,128)S(1)}, bf16[128,256]{1,0:T(8,128)(2,1)S(1)}) custom-call(bf16[128,1024]{1,0:T(8,128)(2,1)} %th_h.1, f32[1,1024]{1,0:T(1,128)} %bitcast.9, bf16[1024,512]{1,0:T(8,128)(2,1)} %pj_h.1, bf16[128,512]{1,0:T(8,128)(2,1)} %sh_h.1, f32[1,512]{1,0:T(1,128)} %bitcast.10, ...), custom_call_target="tpu_custom_call" | custom-call | tf_op jit(solution)/shard_map/pallas_call | solution.py:781
  87.9 0.7 copy.15
  88.6 0.5 copy.16
  89.1 0.6 copy.17

commit v9 on v8

--- a/solution.py
+++ b/solution.py
@@ -618,7 +618,6 @@
     t_place(0)
     for k in range(1, BACK + 1):
         kv_mid(k)
-    rt.relay(1)
 
     lax.fori_loop(1, BACK + 1, kv_got, 0)
     keys = jnp.concatenate([kv_r[0, j] for j in range(BACK + 1)], axis=1)
@@ -632,6 +631,7 @@
         attn_v[c * 2 + h] = (acc / total).astype(BF16)
         send(attn_v.at[c * 2 + h], attn_v.at[c * 2 + h], x_ss.at[5 + h], x_rs.at[5 + h], sib)
     lax.fori_loop(0, 8, wo_got, 0)
+    rt.relay(1)
 
     ro = Reduce((yo_, yh), o_own, None, None, o_x2, o_ra, o_rb, o_xp, o_xm, o_fm, o_fp, o_ys, o_yr, o_fin, o_ss, o_rs)
 

time: 89.8 us -> 90.4 us (level)
  no operation moved by 1% of the time
where the time goes in v9:
time: 90.4 us; the launch traced here: 90.3 us
  Pallas kernels  87.9 us (97%)
  local copies, waits for them, and re-layouts  1.8 us (2%)
    pallas_call x1, Pallas kernels, on_device(): pl.pallas_call(body, out_shape=(jax.ShapeDtypeStruct(block, BF16), jax.Sh...  87.9 us

profile of v9, /device:TPU:1, one launch (start us, length us, event | category | flops | bytes accessed | tf_op | source)
XLA Modules:
  0.0 90.3 jit_solution(16799426910466226878)
XLA Ops:
  0.6 87.9 %shard_map.112 = (bf16[128,512]{1,0:T(8,128)(2,1)S(1)}, f32[1,128]{1,0:T(1,128)S(1)}, bf16[128,256]{1,0:T(8,128)(2,1)S(1)}) custom-call(bf16[128,1024]{1,0:T(8,128)(2,1)} %th_h.1, f32[1,1024]{1,0:T(1,128)} %bitcast.9, bf16[1024,512]{1,0:T(8,128)(2,1)} %pj_h.1, bf16[128,512]{1,0:T(8,128)(2,1)} %sh_h.1, f32[1,512]{1,0:T(1,128)} %bitcast.10, ...), custom_call_target="tpu_custom_call" | custom-call | tf_op jit(solution)/shard_map/pallas_call | solution.py:781
  88.5 0.7 copy.15
  89.2 0.5 copy.16
  89.7 0.6 copy.17
